TPU v7x, 512 devices: a whole 4x8x8 slice. The times are simulated.
512 devices in a mesh: space: 128 (over y, z, core), scene: 4 (over x).
Axes of the slice: x: 4, y: 8, z: 8, core: 2. Of those that a mesh axis runs over, the one named last changes fastest.
Arguments:
- coarse_features: bfloat16 [4, 8192, 128], P('scene', 'space'), may hold values from -6 to 6
- child_counts: int32 [4, 8192], P('scene', 'space'), may hold values from 4 to 8
- neighbour_rows: int32 [4, 27, 65536], P('scene', None, 'space'), may hold values from -1 to 95, as said below
- fine_owners: int32 [4, 65536, 1], P('scene', 'space'), may hold values from 0 to 127; in each aligned block of 512 rows (0 to 511, 512 to 1023, ..., all dimensions but the last counted through in order) at most 6 rows name the same one
- weights: bfloat16 [27, 128, 64], replicated, may hold values from -0.1875 to 0.1875
- cotangent: bfloat16 [4, 16384, 6, 64], P('scene', 'space'), may hold values from -0.75 to 0.75
Outputs:
- fine_out: bfloat16 [4, 16384, 6, 64], P('scene', 'space')
- coarse_grad: bfloat16 [4, 8192, 128], P('scene', 'space')
- weight_grad: float32 [27, 128, 64], replicated
Inputs may be any that keep to these rules, and one draw needn't show every extreme that they name: `neighbour_rows`: A valid row is 16 + c + d for the slot's coarse row c and some d with |d| <= 16; the last slot of a slab names row 95 at offset 0 and the first names row 0 at offset 1. `fine_owners`: within the slots of one device, at most 6 name the same owner, a bound that some block reaches.
All inputs are finite; a program needn't handle non-finite values.
Results may differ from a plain program's by a relative error of at most 0.00105.
Values may be sent and summed in bfloat16 or wider, within the bound.
A program may use at most 64 MiB of HBM per device.

v0:
```python
import jax
import jax.numpy as jnp
from jax import lax
from jax.sharding import PartitionSpec as P


def extended(value, sides, width):
    for axis, dim in sides:
        devices, length = (lax.axis_size(axis), value.shape[dim])
        up = [(i, (i + 1) % devices) for i in range(devices - 1)]
        down = [(j, i) for i, j in up]
        last = lax.slice_in_dim(value, length - width, length, axis=dim)
        initial = lax.slice_in_dim(value, 0, width, axis=dim)
        before = lax.ppermute(last, axis, up)
        after = lax.ppermute(initial, axis, down)
        value = jnp.concatenate([before, value, after], axis=dim)
    return value


def gather_rows(table, rows):
    found = jnp.take(table, jnp.maximum(rows, 0), axis=0)
    return jnp.where((rows >= 0)[:, None], found, jnp.zeros_like(found))


def forward_block(table, rows_all, weights):

    def forward_step(total, item):
        rows, kernel = item
        return (
            total + jnp.dot(gather_rows(table, rows), kernel, preferred_element_type=jnp.float32),
            None,
        )

    start = jnp.zeros((rows_all.shape[1], weights.shape[2]), jnp.float32)
    total, _ = lax.scan(forward_step, start, (rows_all, weights))
    return total


def backward_block(table, rows_all, weights, slot_grad):

    def backward_step(grad_table, item):
        rows, kernel = item
        found = gather_rows(table, rows)
        kernel_grad = lax.dot_general(
            found, slot_grad, (((0,), (0,)), ((), ())), preferred_element_type=jnp.float32
        )
        term = lax.dot_general(
            slot_grad, kernel, (((1,), (1,)), ((), ())), preferred_element_type=jnp.float32
        )
        term = jnp.where((rows >= 0)[:, None], term, jnp.zeros_like(term))
        grad_table = grad_table.at[jnp.maximum(rows, 0)].add(term)
        return (grad_table, kernel_grad)

    start = jnp.zeros((table.shape[0], weights.shape[1]), jnp.float32)
    return lax.scan(backward_step, start, (rows_all, weights))


def slot_ranks(owners, spread):
    slots = owners.shape[0]
    width = min(128, slots)
    onehot = (owners[:, None] == jnp.arange(spread, dtype=jnp.int32)[None, :]).astype(jnp.bfloat16)
    grouped = onehot.reshape(slots // width, width, spread)
    index = jnp.arange(width, dtype=jnp.int32)
    before_mask = (index[:, None] > index[None, :]).astype(jnp.bfloat16)
    within = jnp.einsum("ij,bjs->bis", before_mask, grouped, preferred_element_type=jnp.float32)
    group_totals = jnp.sum(grouped.astype(jnp.float32), axis=1)
    earlier = jnp.cumsum(group_totals, axis=0) - group_totals
    counted = (within + earlier[:, None, :]).reshape(slots, spread)
    return jnp.sum(counted * onehot.astype(jnp.float32), axis=1).astype(jnp.int32)


def on_device(coarse_features, child_counts, neighbour_rows, fine_owners, weights, cotangent):
    spread = lax.axis_size("space")
    feats = coarse_features[0]
    counts = child_counts[0]
    rows_all = neighbour_rows[0]
    owners = fine_owners[0, :, 0]
    rim_rows = feats.shape[0] // 4
    slots = rows_all.shape[1]
    table = extended(feats, (("space", 0),), rim_rows)
    valid = (jnp.arange(8, dtype=jnp.int32)[None, :] < counts[:, None]).reshape(slots)
    totals = forward_block(table, rows_all, weights)
    slot_out = jnp.where(valid[:, None], totals, jnp.zeros_like(totals)).astype(jnp.bfloat16)
    ranks = slot_ranks(owners, spread)
    capacity = cotangent.shape[2]
    channels = slot_out.shape[1]
    target = owners * capacity + ranks
    outgoing = jnp.zeros((spread * capacity, channels), jnp.bfloat16).at[target].set(slot_out)
    outgoing = outgoing.reshape(spread, capacity, channels)
    arrived = lax.all_to_all(outgoing, "space", split_axis=0, concat_axis=0, tiled=True)
    returned = lax.all_to_all(cotangent[0], "space", split_axis=0, concat_axis=0, tiled=True)
    slot_grad = jnp.take(returned.reshape(spread * capacity, channels), target, axis=0)
    slot_grad = jnp.where(valid[:, None], slot_grad, jnp.zeros_like(slot_grad))
    grad_table, kernel_grads = backward_block(table, rows_all, weights, slot_grad)
    rims = jnp.concatenate([grad_table[:rim_rows], grad_table[-rim_rows:]], axis=0)
    beside = extended(rims, (("space", 0),), rim_rows)
    own = grad_table[rim_rows:-rim_rows]
    own = own.at[:rim_rows].add(beside[:rim_rows])
    own = own.at[-rim_rows:].add(beside[-rim_rows:])
    weight_grad = lax.psum(kernel_grads, ("space", "scene"))
    return (arrived[None], own.astype(jnp.bfloat16)[None], weight_grad)


def solution(mesh):
    return jax.shard_map(
        on_device,
        mesh=mesh,
        in_specs=(
            P("scene", "space", None),
            P("scene", "space"),
            P("scene", None, "space"),
            P("scene", "space", None),
            P(),
            P("scene", "space", None, None),
        ),
        out_specs=(P("scene", "space", None, None), P("scene", "space", None), P()),
        check_vma=False,
    )
```

profile of v0, /device:TPU:1, one launch (start us, length us, event | category | flops | bytes accessed | tf_op | source)
XLA Modules:
  0.0 598.4 jit_solution(10330985500326128020)
XLA Ops:
  9.1 18.6 %all-to-all-start.1 = ((bf16[128,2,192]{2,1,0:T(2,128)(2,1)}), bf16[128,2,192]{2,1,0:T(2,128)(2,1)S(1)}, u32[]{:S(2)}, u32[]{:S(2)}) async-start(bf16[128,2,192]{2,1,0:T(2,128)(2,1)} %reshape.252), calls=%async_computation.1 | async-start | bytes 262144 | tf_op jit(solution)/shard_map/all_to_all | solution.py:91
  27.7 3.5 collective-permute-start
  31.2 1.9 collective-permute-start.1
  34.5 2.0 collective-permute-done.1
  36.5 68.9 %while.26 = (s32[]{:T(128)}, f32[512,64]{0,1:T(8,128)S(1)}, s32[27,512]{1,0:T(8,128)S(1)}, bf16[96,128]{1,0:T(8,128)(2,1)S(1)}, bf16[27,128,64]{1,2,0:T(8,128)(2,1)}, /*index=5*/s32[]{:T(128)}, s32[]{:T(128)}) while((s32[]{:T(128)}, f32[512,64]{0,1:T(8,128)S(1)}, s32[27,512]{1,0:T(8,128)S(1)}, bf16[96,128]{1,0:T(8,128)(2,1)S(1)}, ...), condition=%wide.region_4.6_spmd.clone, body=%wide.region_3.5_spmd.clone.sunk | while | flops 8591875 | bytes 694879 | solution.py:35
  36.5 1.3 gather_fusion.1
  39.1 1.3 gather_fusion.1
  41.6 1.3 gather_fusion.1
  44.2 1.3 gather_fusion.1
  46.7 1.3 gather_fusion.1
  49.3 1.3 gather_fusion.1
  51.8 1.3 gather_fusion.1
  54.4 1.3 gather_fusion.1
  56.9 1.3 gather_fusion.1
  59.5 1.3 gather_fusion.1
  62.0 1.3 gather_fusion.1
  64.6 1.3 gather_fusion.1
  67.1 1.3 gather_fusion.1
  69.7 1.3 gather_fusion.1
  74.8 1.3 gather_fusion.1
  100.3 1.3 gather_fusion.1
  102.9 1.3 gather_fusion.1
  105.5 1.9 scatter_custom_fusion.1
  108.4 13.3 %all-to-all-start = ((bf16[128,2,192]{2,1,0:T(2,128)(2,1)}), bf16[128,2,192]{2,1,0:T(2,128)(2,1)S(1)}, u32[]{:S(2)}, u32[]{:S(2)}) async-start(bf16[128,2,192]{2,1,0:T(2,128)(2,1)} %reshape.250), calls=%async_computation | async-start | bytes 262144 | tf_op jit(solution)/shard_map/all_to_all | solution.py:90
  122.0 1.3 gather_fusion.2
  123.6 185.6 %while.25 = (s32[]{:T(128)}, f32[96,128]{1,0:T(8,128)S(1)}, f32[27,128,64]{1,2,0:T(8,128)}, s32[27,512]{1,0:T(8,128)S(1)}, bf16[27,128,64]{1,2,0:T(8,128)(2,1)},...) while((s32[]{:T(128)}, f32[96,128]{1,0:T(8,128)S(1)}, f32[27,128,64]{1,2,0:T(8,128)}, ...), condition=%wide.region_8.10_spmd, body=%wide.region_6.9_spmd.sunk | while | flops 17046016 | bytes 2172509 | solution.py:55
  123.7 1.3 gather_fusion
  127.1 3.3 scatter_fusion
  134.0 3.4 scatter_fusion
  140.8 3.4 scatter_fusion
  147.7 3.4 scatter_fusion
  154.6 3.4 scatter_fusion
  161.5 3.3 scatter_fusion
  168.3 3.4 scatter_fusion
  171.8 1.3 gather_fusion
  175.2 3.4 scatter_fusion
  182.1 3.3 scatter_fusion
  188.9 3.4 scatter_fusion
  195.8 3.4 scatter_fusion
  202.7 3.4 scatter_fusion
  209.5 3.4 scatter_fusion
  213.0 1.3 gather_fusion
  216.4 3.4 scatter_fusion
  223.3 3.4 scatter_fusion
  226.8 1.3 gather_fusion
  230.2 3.4 scatter_fusion
  237.1 3.4 scatter_fusion
  244.0 3.4 scatter_fusion
  250.9 3.4 scatter_fusion
  257.7 3.4 scatter_fusion
  264.6 3.5 scatter_fusion
  271.6 3.3 scatter_fusion
  278.4 3.3 scatter_fusion
  285.3 3.4 scatter_fusion
  292.2 3.4 scatter_fusion
  295.6 1.3 gather_fusion
  299.0 3.3 scatter_fusion
  302.4 1.3 gather_fusion
  305.8 3.3 scatter_fusion
  309.2 3.3 collective-permute-start.2
  312.5 1.9 collective-permute-start.3
  315.5 2.0 collective-permute-done.3
  318.1 271.3 %all-reduce.2.cloned.1.call-done = f32[27,128,64]{1,2,0:T(8,128)} async-done(((f32[27,128,64]{1,2,0:T(8,128)}), f32[27,128,64]{1,2,0:T(8,128)}) %all-reduce.2.cloned.1.call-update) | async-done | bytes 884752 | tf_op jit(solution)/shard_map/psum | solution.py:100
  589.4 2.2 copy.46
  (455 shorter events, 135.3 us)
Async XLA Ops:
  9.1 18.6 %copy-start.1 = (bf16[1,64,128]{2,1,0:T(8,128)(2,1)S(1)}, bf16[1,64,128]{2,1,0:T(8,128)(2,1)}, u32[]{:S(2)}) copy-start(bf16[1,64,128]{2,1,0:T(8,128)(2,1)} %param.16) | copy-start | bytes 49156
  9.1 99.3 %all-to-all-start.1 = ((bf16[128,2,192]{2,1,0:T(2,128)(2,1)}), bf16[128,2,192]{2,1,0:T(2,128)(2,1)S(1)}, u32[]{:S(2)}, u32[]{:S(2)}) async-start(bf16[128,2,192]{2,1,0:T(2,128)(2,1)} %reshape.252), calls=%async_computation.1 | async-start | bytes 262144 | tf_op jit(solution)/shard_map/all_to_all | solution.py:91
  27.7 5.5 copy-start.2
  27.7 6.8 %collective-permute-start = (bf16[16,128]{1,0:T(8,128)(2,1)S(1)}, bf16[16,128]{1,0:T(8,128)(2,1)S(1)}, u32[]{:S(2)}, u32[]{:S(2)}) collective-permute-start(bf16[16,128]{1,0:T(8,128)(2,1)S(1)} %get-tuple-element.146), channel_id=1, source_target_pairs={{0,4},{4,8},{8,12},{12,16},{16,20},{20,24},{24,28},{28,32},{32,36}... | collective-permute-start | bytes 12296 | tf_op jit(solution)/shard_map/ppermute | solution.py:14
  31.2 5.2 collective-permute-start.1
  33.4 1.1 copy-start
  33.6 0.7 copy-start.3
  108.4 206.1 %all-to-all-start = ((bf16[128,2,192]{2,1,0:T(2,128)(2,1)}), bf16[128,2,192]{2,1,0:T(2,128)(2,1)S(1)}, u32[]{:S(2)}, u32[]{:S(2)}) async-start(bf16[128,2,192]{2,1,0:T(2,128)(2,1)} %reshape.250), calls=%async_computation | async-start | bytes 262144 | tf_op jit(solution)/shard_map/all_to_all | solution.py:90
  121.7 467.7 %all-reduce.2.cloned.1.call-start = ((), (), s32[]{:S(2)}) async-start(), calls=%async_computation.2 | async-start | bytes 1769472 | tf_op jit(solution)/shard_map/psum | solution.py:100
  309.2 6.3 %collective-permute-start.2 = (f32[16,128]{1,0:T(8,128)S(1)}, f32[16,128]{1,0:T(8,128)S(1)}, u32[]{:S(2)}, u32[]{:S(2)}) collective-permute-start(f32[16,128]{1,0:T(8,128)S(1)} %get-tuple-element.145), channel_id=1, source_target_pairs={{0,4},{4,8},{8,12},{12,16},{16,20},{20,24},{24,28},{28,32},{32,36}... | collective-permute-start | bytes 24584 | tf_op jit(solution)/shard_map/ppermute | solution.py:14
  312.5 5.0 collective-permute-start.3
Sparse Core Ops, SparseCore 0:
  314.6 274.7 all-reduce.1
where the time goes:
time: 604 us; the launch traced here: 598 us
  waiting for transfers between devices  275 us (46%)
  other arithmetic  97.1 us (16%)
  local copies, waits for them, and re-layouts  84.3 us (14%)
  matrix products  81.1 us (13%)
  starting transfers between devices  42.6 us (7%)
  between operations  14.3 us (2%)
    psum x1, waiting for transfers between devices, on_device(): weight_grad = lax.psum(kernel_grads, ('space', 'scene'))  271 us
    scatter-add x27, other arithmetic, backward_step(): grad_table = grad_table.at[jnp.maximum(rows, 0)].add(term)  90.9 us
    gather x54, local copies, waits for them, and re-layouts, gather_rows(): found = jnp.take(table, jnp.maximum(rows, 0), axis=0)  72.4 us
    dot_general x27, matrix products, forward_step(): jnp.dot(gather_rows(table, rows), kernel, preferred_element_type=jnp.floa...  29.3 us
    dot_general x27, matrix products, backward_step(): lax.dot_general(found, slot_grad, (((0,), (0,)), ((), ())), preferred_ele...  26.7 us
    dot_general x27, matrix products, backward_step(): lax.dot_general(slot_grad, kernel, (((1,), (1,)), ((), ())), preferred_el...  24.8 us
    all_to_all x1, starting transfers between devices, on_device(): lax.all_to_all(cotangent[0], 'space', split_axis=0, concat_axis=0, tiled=...  18.6 us
    all_to_all x1, starting transfers between devices, on_device(): lax.all_to_all(outgoing, 'space', split_axis=0, concat_axis=0, tiled=True)  13.3 us
  transfers between devices with their start and end apart: 7, of which 3 were waited for; matrix products, arithmetic and copies ran while one was open for 43% of the time, Pallas kernels for 0%

commit v1 on v0

v1 whole, which is shorter than its diff:
```python
import jax
import jax.numpy as jnp
from jax import lax
from jax.experimental import pallas as pl
from jax.experimental.pallas import tpu as pltpu
from jax.sharding import PartitionSpec as P

KVOL, CIN, COUT = 27, 128, 64
SLOTS, COARSE, HALO, CAP = 512, 64, 16, 6
NY, NZ, NC, NX = 8, 8, 2, 4
NJ = NZ * NC
NS = NY * NJ
TAB = 128
WIDE = CAP * COUT
ROWS = KVOL * COUT
HALF = ROWS // NC
QUART = HALF // NX
PART = 32
MESH = pl.DeviceIdType.MESH
F32, BF16 = jnp.float32, jnp.bfloat16


def dot(a, b, dims):
    return lax.dot_general(a, b, (dims, ((), ())), preferred_element_type=F32)


def nn(a, b):
    return dot(a, b, ((1,), (0,)))


def nt(a, b):
    return dot(a, b, ((1,), (1,)))


def split(value):
    high = value.astype(BF16)
    return high, (value - high.astype(F32)).astype(BF16)


def iota(shape, dim):
    return lax.broadcasted_iota(jnp.int32, shape, dim)


def kernel(
    feats, counts, rows, owners, weights, cot,
    fine, coarse, wgrad,
    table, onehot, place, wt, zz, st,
    c1, c2s, c2, f1s, f1, f2s,
    grad, rim_low, rim_high,
    w0, l1, a1, l2, a2, l3, a3, l4, b3, g3, g2,
    y_send, y_recv, j_send, j_recv, e_send, e_recv,
    z_send, z_recv, x_send, x_recv, p_send, p_recv,
):
    s, x = lax.axis_index("space"), lax.axis_index("scene")
    y, j = s // NJ, s % NJ
    z, c = j // NC, j % NC
    up, down = (s + 1) % NS, (s + NS - 1) % NS
    partner = y * NJ + z * NC + 1 - c

    def at(space, scene=None):
        return {"space": space, "scene": x if scene is None else scene}

    def y_peer(p):
        return (y + p) % NY

    def j_peer(p):
        return (j + p) % NJ

    def z_peer(p):
        return (z + p) % NZ

    def x_peer(p):
        return (x + p) % NX

    started = []

    def send(src, dst, send_sem, recv_sem, device):
        copy = pltpu.make_async_remote_copy(
            src_ref=src, dst_ref=dst, send_sem=send_sem, recv_sem=recv_sem,
            device_id=device, device_id_type=MESH,
        )
        copy.start()
        started.append(copy)
        return copy

    def over_y(n, src, dst):
        return [
            send(src(y_peer(p)), dst, y_send.at[n, p], y_recv.at[n, p], at(y_peer(p) * NJ + j))
            for p in range(1, NY)
        ]

    def over_j(n, src, dst):
        return [
            send(src(j_peer(p)), dst, j_send.at[n, p], j_recv.at[n, p], at(y * NJ + j_peer(p)))
            for p in range(1, NJ)
        ]

    def over_z(n, src, dst):
        return [
            send(src(z_peer(p)), dst, z_send.at[n, p], z_recv.at[n, p], at(y * NJ + z_peer(p) * NC + c))
            for p in range(1, NZ)
        ]

    def over_x(n, src, dst):
        return [
            send(src(x_peer(p)), dst, x_send.at[n, p], x_recv.at[n, p], at(s, x_peer(p)))
            for p in range(1, NX)
        ]

    def arrived(copies):
        for copy in copies:
            copy.wait_recv()

    barrier = pltpu.get_barrier_semaphore()
    peers = [at(y_peer(p) * NJ + j) for p in range(1, NY)]
    peers += [at(y * NJ + j_peer(p)) for p in range(1, NJ)]
    peers += [at(s, x_peer(p)) for p in range(1, NX)]
    peers += [at(up), at(down)]
    for peer in peers:
        pl.semaphore_signal(barrier, inc=1, device_id=peer, device_id_type=MESH)
    table[pl.ds(HALO, COARSE), :] = feats[...]
    table[pl.ds(HALO + COARSE + HALO, TAB - COARSE - 2 * HALO), :] = jnp.zeros(
        (TAB - COARSE - 2 * HALO, CIN), BF16
    )
    pl.semaphore_wait(barrier, len(peers))

    cot_first = over_y(0, lambda d: cot.at[d], c1.at[y])
    halo_up = send(
        feats.at[pl.ds(COARSE - HALO, HALO)], table.at[pl.ds(0, HALO)],
        e_send.at[0], e_recv.at[0], at(up),
    )
    halo_down = send(
        feats.at[pl.ds(0, HALO)], table.at[pl.ds(HALO + COARSE, HALO)],
        e_send.at[1], e_recv.at[1], at(down),
    )
    c1[y] = cot[y]

    line = iota((TAB, SLOTS), 0)
    owner_of = (line & (NY - 1)) * NJ + (line >> 3)
    named = owner_of == owners[...]
    named_bf = jnp.where(named, 1.0, 0.0).astype(BF16)
    earlier = jnp.where(iota((SLOTS, SLOTS), 0) < iota((SLOTS, SLOTS), 1), 1.0, 0.0).astype(BF16)
    before = nn(named_bf, earlier)
    for r in range(CAP):
        place[pl.ds(r * TAB, TAB), :] = jnp.where(named & (before == r), 1.0, 0.0).astype(BF16)
    spread = jnp.where(iota((COARSE, SLOTS), 0) == (iota((COARSE, SLOTS), 1) >> 3), 1.0, 0.0).astype(BF16)
    many = jnp.broadcast_to(counts[...], (8, COARSE)).astype(F32).astype(BF16)
    limit = nn(many, spread)[0:1]
    valid = (iota((1, SLOTS), 1) & 7).astype(F32) < limit
    for k in range(KVOL):
        onehot[pl.ds(k * TAB, TAB), :] = jnp.where(line == rows[pl.ds(k, 1), :], 1.0, 0.0).astype(BF16)
        wt[pl.ds(k * COUT, COUT), :] = weights[k].T

    square = (TAB, TAB)
    to_j = jnp.where(
        iota(square, 1) == (iota(square, 0) & (NY - 1)) * NJ + (iota(square, 0) >> 3), 1.0, 0.0
    ).astype(BF16)
    to_y = jnp.where(
        iota(square, 1) == (iota(square, 0) & (NJ - 1)) * NY + (iota(square, 0) >> 4), 1.0, 0.0
    ).astype(BF16)

    arrived(cot_first)
    c2s[...] = nn(to_j, c1[...].reshape(NS, WIDE)).reshape(NJ, NY, WIDE).astype(BF16)
    cot_second = over_j(0, lambda d: c2s.at[d], c2.at[j])
    c2[j] = c2s[j]

    arrived([halo_up, halo_down])

    @pl.when(s == 0)
    def _():
        table[pl.ds(0, HALO), :] = jnp.zeros((HALO, CIN), BF16)

    @pl.when(s == NS - 1)
    def _():
        table[pl.ds(HALO + COARSE, HALO), :] = jnp.zeros((HALO, CIN), BF16)

    features = table[...]
    for k in range(KVOL):
        high, low = split(nt(wt[pl.ds(k * COUT, COUT), :], features))
        zz[pl.ds(0, COUT), pl.ds(k * TAB, TAB)] = high
        zz[pl.ds(COUT, COUT), pl.ds(k * TAB, TAB)] = low
    both = nn(zz[...], onehot[...])
    slot_out = jnp.where(valid, both[:COUT] + both[COUT:], 0.0).astype(BF16)
    for r in range(CAP):
        f1s[:, :, pl.ds(r * COUT, COUT)] = (
            nt(place[pl.ds(r * TAB, TAB), :], slot_out).reshape(NJ, NY, COUT).astype(BF16)
        )
    fine_first = over_j(1, lambda d: f1s.at[d], f1.at[j])
    f1[j] = f1s[j]

    arrived(cot_second)
    turned = c2[...].astype(F32).reshape(NS, WIDE).T.astype(BF16)
    turned = jnp.concatenate([turned[r * COUT:(r + 1) * COUT] for r in range(CAP)], axis=1)
    slot_grad = jnp.where(valid, nn(turned, place[...]), 0.0).astype(BF16)
    for k in range(KVOL):
        high, low = split(nt(slot_grad, onehot[pl.ds(k * TAB, TAB), :]))
        st[pl.ds(k * COUT, COUT), pl.ds(0, TAB)] = high
        st[pl.ds(k * COUT, COUT), pl.ds(TAB, TAB)] = low
    twice = jnp.concatenate([features, features], axis=0)
    w0[1 - c] = nn(st[pl.ds(pl.multiple_of((1 - c) * HALF, 16), HALF), :], twice)
    reduce_core = send(w0.at[1 - c], l1, p_send.at[0], p_recv.at[0], at(partner))
    w0[c] = nn(st[pl.ds(pl.multiple_of(c * HALF, 16), HALF), :], twice)

    total = jnp.zeros((CIN, 2 * TAB), F32)
    for k in range(KVOL):
        total = total + nn(weights[k], st[pl.ds(k * COUT, COUT), :])
    grad[...] = (total[:, :TAB] + total[:, TAB:]).T
    rim_down = send(grad.at[pl.ds(0, HALO)], rim_high, e_send.at[2], e_recv.at[2], at(down))
    rim_up = send(
        grad.at[pl.ds(HALO + COARSE, HALO)], rim_low, e_send.at[3], e_recv.at[3], at(up)
    )

    arrived([reduce_core])
    for q in range(NX):
        a1[q] = w0[c, pl.ds(q * QUART, QUART), :] + l1[pl.ds(q * QUART, QUART), :]
    reduce_x = over_x(0, lambda d: a1.at[d], l2.at[x])

    arrived(fine_first)
    f2s[...] = (
        nn(to_y, f1[...].astype(F32).reshape(NS, WIDE).astype(BF16)).astype(BF16).reshape(NY, NJ, WIDE)
    )
    fine_second = over_y(1, lambda d: f2s.at[d], fine.at[y])
    fine[y] = f2s[y]

    a2[pl.ds(QUART, NZ * PART - QUART), :] = jnp.zeros((NZ * PART - QUART, CIN), F32)
    arrived(reduce_x)
    mine = a1[x]
    for p in range(1, NX):
        mine = mine + l2[x_peer(p)]
    a2[pl.ds(0, QUART), :] = mine

    def part(ref, d):
        return ref.at[pl.ds(pl.multiple_of(d * PART, PART), PART)]

    reduce_z = over_z(0, lambda d: part(a2, d), l3.at[z])

    arrived([rim_down, rim_up])
    own = grad[pl.ds(HALO, COARSE), :]
    low = rim_low[...] * jnp.where(s == 0, 0.0, 1.0)
    high = rim_high[...] * jnp.where(s == NS - 1, 0.0, 1.0)
    coarse[pl.ds(0, HALO), :] = (own[:HALO] + low).astype(BF16)
    coarse[pl.ds(HALO, COARSE - 2 * HALO), :] = own[HALO:COARSE - HALO].astype(BF16)
    coarse[pl.ds(COARSE - HALO, HALO), :] = (own[COARSE - HALO:] + high).astype(BF16)

    arrived(reduce_z)
    mine = part(a2, z)[...]
    for p in range(1, NZ):
        mine = mine + l3[z_peer(p)]
    a3[...] = mine
    gather_y = over_y(2, lambda d: a3, l4.at[y])
    l4[y] = mine
    arrived(gather_y)
    done = l4[0]
    for q in range(1, NY):
        done = done + l4[q]
    b3[...] = done
    gather_z = over_z(1, lambda d: b3, part(g3, z))
    part(g3, z)[...] = done
    arrived(gather_z)
    gather_x = over_x(1, lambda d: g3.at[pl.ds(0, QUART)], g2.at[x])
    g2[x] = g3[pl.ds(0, QUART), :]
    arrived(gather_x)
    gather_core = send(g2, wgrad.at[c], p_send.at[1], p_recv.at[1], at(partner))
    wgrad[c] = g2[...]
    arrived([gather_core])
    arrived(fine_second)
    for copy in started:
        copy.wait_send()


def on_device(coarse_features, child_counts, neighbour_rows, fine_owners, weights, cotangent):
    vmem = pl.BlockSpec(memory_space=pltpu.VMEM)
    sem = pltpu.SemaphoreType.DMA
    fine, coarse, wgrad = pl.pallas_call(
        kernel,
        out_shape=(
            jax.ShapeDtypeStruct((NY, NJ, WIDE), BF16),
            jax.ShapeDtypeStruct((COARSE, CIN), BF16),
            jax.ShapeDtypeStruct((NC, NX, QUART, CIN), F32),
        ),
        in_specs=[vmem] * 6,
        out_specs=(vmem, vmem, vmem),
        scratch_shapes=[
            pltpu.VMEM((TAB, CIN), BF16),
            pltpu.VMEM((KVOL * TAB, SLOTS), BF16),
            pltpu.VMEM((CAP * TAB, SLOTS), BF16),
            pltpu.VMEM((ROWS, CIN), BF16),
            pltpu.VMEM((2 * COUT, KVOL * TAB), BF16),
            pltpu.VMEM((ROWS, 2 * TAB), BF16),
            pltpu.VMEM((NY, NJ, WIDE), BF16),
            pltpu.VMEM((NJ, NY, WIDE), BF16),
            pltpu.VMEM((NJ, NY, WIDE), BF16),
            pltpu.VMEM((NJ, NY, WIDE), BF16),
            pltpu.VMEM((NJ, NY, WIDE), BF16),
            pltpu.VMEM((NY, NJ, WIDE), BF16),
            pltpu.VMEM((TAB, CIN), F32),
            pltpu.VMEM((HALO, CIN), F32),
            pltpu.VMEM((HALO, CIN), F32),
            pltpu.VMEM((NC, HALF, CIN), F32),
            pltpu.VMEM((HALF, CIN), F32),
            pltpu.VMEM((NX, QUART, CIN), F32),
            pltpu.VMEM((NX, QUART, CIN), F32),
            pltpu.VMEM((NZ * PART, CIN), F32),
            pltpu.VMEM((NZ, PART, CIN), F32),
            pltpu.VMEM((PART, CIN), F32),
            pltpu.VMEM((NY, PART, CIN), F32),
            pltpu.VMEM((PART, CIN), F32),
            pltpu.VMEM((NZ * PART, CIN), F32),
            pltpu.VMEM((NX, QUART, CIN), F32),
            sem((3, NY)), sem((3, NY)),
            sem((2, NJ)), sem((2, NJ)),
            sem((4,)), sem((4,)),
            sem((2, NZ)), sem((2, NZ)),
            sem((2, NX)), sem((2, NX)),
            sem((2,)), sem((2,)),
        ],
        compiler_params=pltpu.CompilerParams(
            collective_id=0, has_side_effects=True, vmem_limit_bytes=48 * 1024 * 1024
        ),
        cost_estimate=pl.CostEstimate(flops=2_000_000_000, bytes_accessed=4_000_000, transcendentals=0),
    )(
        coarse_features[0],
        child_counts,
        neighbour_rows[0],
        fine_owners.reshape(1, SLOTS),
        weights,
        cotangent.reshape(NY, NJ, WIDE),
    )
    return (
        fine.reshape(1, NS, CAP, COUT),
        coarse[None],
        wgrad.reshape(KVOL, COUT, CIN).transpose(0, 2, 1),
    )


def solution(mesh):
    return jax.shard_map(
        on_device,
        mesh=mesh,
        in_specs=(
            P("scene", "space", None),
            P("scene", "space"),
            P("scene", None, "space"),
            P("scene", "space", None),
            P(),
            P("scene", "space", None, None),
        ),
        out_specs=(P("scene", "space", None, None), P("scene", "space", None), P()),
        check_vma=False,
    )
```

time: 604 us -> 69.7 us (0.12)
  waiting for transfers between devices: 275 us -> 0 us
  other arithmetic: 97.1 us -> 0 us
  matrix products: 81.1 us -> 0 us
  local copies, waits for them, and re-layouts: 84.3 us -> 4.48 us
  Pallas kernels: 0 us -> 64.3 us
  starting transfers between devices: 42.6 us -> 0 us
  between operations: 14.3 us -> 0.7 us
    psum x1 -> x0, waiting for transfers between devices: 271 us -> none  [on_device(): weight_grad = lax.psum(kernel_grads, ('space', 'scene'))]
    scatter-add x29 -> x0, other arithmetic: 90.9 us -> none  [the longest x27 90.9 us: backward_step(): grad_table = grad_table.at[jnp.maximum(rows, 0)].add(term)]
    dot_general x82 -> x0, matrix products: 81.1 us -> none  [the longest x27 29.3 us: forward_step(): jnp.dot(gather_rows(table, rows), kernel, preferred_element_type=jnp.floa...]
    gather x55 -> x0, local copies, waits for them, and re-layouts: 73.7 us -> none  [the longest x54 72.4 us: gather_rows(): found = jnp.take(table, jnp.maximum(rows, 0), axis=0)]
    pallas_call x0 -> x1, Pallas kernels: none -> 64.3 us  [on_device(): pl.pallas_call(kernel, out_shape=(jax.ShapeDtypeStruct((NY, NJ, WIDE), BF...]
    all_to_all x2 -> x0, starting transfers between devices: 31.8 us -> none  [the longest x1 18.6 us: on_device(): lax.all_to_all(cotangent[0], 'space', split_axis=0, concat_axis=0, tiled=...]
    ppermute x4 -> x0, starting transfers between devices: 10.7 us -> none  [the longest x2 6.85 us: extended(): before = lax.ppermute(last, axis, up)]
  transfers between devices with their start and end apart: 7 -> 0, of which waited for: 3 -> 0; matrix products, arithmetic and copies ran while one was open for 43% -> 0% of each run, Pallas kernels for 0% -> 0%
where the time goes in v1:
time: 69.7 us; the launch traced here: 69.5 us
  Pallas kernels  64.3 us (92%)
  local copies, waits for them, and re-layouts  4.48 us (6%)
  between operations  0.7 us (1%)
    pallas_call x1, Pallas kernels, on_device(): pl.pallas_call(kernel, out_shape=(jax.ShapeDtypeStruct((NY, NJ, WIDE), BF...  64.3 us
    unnamed x16, local copies, waits for them, and re-layouts  4.1 us

profile of v1, /device:TPU:1, one launch (start us, length us, event | category | flops | bytes accessed | tf_op | source)
XLA Modules:
  0.0 69.5 jit_solution(8456146415334407529)
XLA Ops:
  0.6 0.0 copy-start.4
  0.6 0.0 copy-start.3
  0.7 0.9 %copy.17 = s32[1,27,512]{2,1,0:T(8,128)S(1)} copy(s32[1,27,512]{2,0,1:T(1,128)} %param.8) | data formatting | bytes 110592
  1.5 0.0 copy-done.4
  1.5 0.2 copy.12
  1.7 0.2 reshape.19.cot
  1.9 0.0 copy-done.3
  1.9 0.0 copy-start
  2.0 0.0 copy-start.1
  2.0 0.0 copy-start.2
  2.0 0.4 copy.13.weights
  2.4 0.2 copy-done
  2.7 0.0 copy-done.1
  2.7 0.0 copy-done.2
  2.7 64.3 %shard_map.85 = (bf16[8,16,384]{2,1,0:T(8,128)(2,1)S(1)}, bf16[64,128]{1,0:T(8,128)(2,1)S(1)}, f32[2,4,216,128]{3,2,1,0:T(8,128)S(1)}) custom-call(bf16[64,128]{1,0:T(8,128)(2,1)S(1)} %bitcast.12, s32[1,64]{1,0:T(1,128)S(1)} %copy-done.2, s32[27,512]{1,0:T(8,128)S(1)} %bitcast.10, s32[1,512]{1,0:T(1,128)S(1)} %bitcast.13, ...), custom_call_target="tpu_custom_call" | custom-call | flops 2000000000 | bytes 4000000 | tf_op jit(solution)/shard_map/pallas_call | solution.py:274
  67.0 0.2 reshape.20
  67.2 0.8 %copy.14 = bf16[1,128,6,64]{1,3,2,0:T(8,128)(2,1)} copy(bf16[1,128,6,64]{3,2,1,0:T(8,128)(2,1)S(1)} %reshape.20) | data formatting | bytes 196608
  68.0 0.6 copy.20
  68.6 0.9 %copy.21 = f32[27,128,64]{1,2,0:T(8,128)} copy(f32[27,128,64]{1,2,0:T(8,128)S(1)} %bitcast.9) | data formatting | bytes 1769472
Async XLA Ops:
  0.6 0.9 %copy-start.4 = (bf16[1,128,6,64]{1,3,2,0:T(8,128)(2,1)S(1)}, bf16[1,128,6,64]{1,3,2,0:T(8,128)(2,1)}, u32[]{:S(2)}) copy-start(bf16[1,128,6,64]{1,3,2,0:T(8,128)(2,1)} %param.11) | copy-start | bytes 294916
  0.6 1.3 %copy-start.3 = (bf16[27,128,64]{1,2,0:T(8,128)(2,1)S(1)}, bf16[27,128,64]{1,2,0:T(8,128)(2,1)}, u32[]{:S(2)}) copy-start(bf16[27,128,64]{1,2,0:T(8,128)(2,1)} %param.10) | copy-start | bytes 1327108
  1.9 0.7 %copy-start = (bf16[1,64,128]{2,1,0:T(8,128)(2,1)S(1)}, bf16[1,64,128]{2,1,0:T(8,128)(2,1)}, u32[]{:S(2)}) copy-start(bf16[1,64,128]{2,1,0:T(8,128)(2,1)} %param.6) | copy-start | bytes 49156
  2.0 0.7 %copy-start.1 = (s32[1,512,1]{1,2,0:T(1,128)S(1)}, s32[1,512,1]{1,2,0:T(1,128)}, u32[]{:S(2)}) copy-start(s32[1,512,1]{1,2,0:T(1,128)} %param.9) | copy-start | bytes 6148
  2.0 0.7 %copy-start.2 = (s32[1,64]{1,0:T(1,128)S(1)}, s32[1,64]{1,0:T(1,128)}, u32[]{:S(2)}) copy-start(s32[1,64]{1,0:T(1,128)} %counts.1) | copy-start | bytes 772

commit v2 on v1

v2 whole, which is shorter than its diff:
```python
import jax
import jax.numpy as jnp
from jax import lax
from jax.experimental import pallas as pl
from jax.experimental.pallas import tpu as pltpu
from jax.sharding import PartitionSpec as P

KVOL, CIN, COUT = 27, 128, 64
SLOTS, COARSE, HALO, CAP = 512, 64, 16, 6
NY, NZ, NC, NX = 8, 8, 2, 4
NJ = NZ * NC
NS = NY * NJ
TAB = 128
WIDE = CAP * COUT
ROWS = KVOL * COUT
HALF = ROWS // NC
PART = 16
PARTS_B = 3
ROWS_A = NX * NZ * PART
ROWS_B = NZ * PARTS_B * PART
MESH = pl.DeviceIdType.MESH
F32, BF16 = jnp.float32, jnp.bfloat16


def dot(a, b, dims):
    return lax.dot_general(a, b, (dims, ((), ())), preferred_element_type=F32)


def nn(a, b):
    return dot(a, b, ((1,), (0,)))


def nt(a, b):
    return dot(a, b, ((1,), (1,)))


def split(value):
    high = value.astype(BF16)
    return high, (value - high.astype(F32)).astype(BF16)


def iota(shape, dim):
    return lax.broadcasted_iota(jnp.int32, shape, dim)


def kernel(
    feats, counts_in, rows_in, owners_in, wt_in, cot_in,
    fine_out, coarse_out, wgrad_out,
    fine, coarse, out_a, out_b,
    counts, rows, owners, wt, cot,
    table, onehot, place, zz, st,
    c1s, c1, c2s, c2, f1s, f1, f2s, f2,
    grad, rim_low, rim_high,
    core_a, from_core_a, core_b, from_core_b,
    x_a, from_x_a, z_a, from_z_a, y_a, from_y_a, done_a, all_z_a,
    z_b, from_z_b, x_b, from_x_b, y_b, from_y_b, done_b, all_x_b,
    y_send, y_recv, j_send, j_recv, e_send, e_recv,
    z_send, z_recv, x_send, x_recv, p_send, p_recv, in_sems, out_sems,
):
    s, x = lax.axis_index("space"), lax.axis_index("scene")
    y, j = s // NJ, s % NJ
    z, c = j // NC, j % NC
    up, down = (s + 1) % NS, (s + NS - 1) % NS
    partner = y * NJ + z * NC + 1 - c

    def at(space, scene=None):
        return {"space": space, "scene": x if scene is None else scene}

    def y_peer(p):
        return (y + p) % NY

    def j_peer(p):
        return (j + p) % NJ

    def z_peer(p):
        return (z + p) % NZ

    def x_peer(p):
        return (x + p) % NX

    started = []

    def send(src, dst, send_sem, recv_sem, device):
        copy = pltpu.make_async_remote_copy(
            src_ref=src, dst_ref=dst, send_sem=send_sem, recv_sem=recv_sem,
            device_id=device, device_id_type=MESH,
        )
        copy.start()
        started.append(copy)
        return copy

    def over_y(n, src, dst):
        return [
            send(src(y_peer(p)), dst, y_send.at[n, p], y_recv.at[n, p], at(y_peer(p) * NJ + j))
            for p in range(1, NY)
        ]

    def over_j(n, src, dst):
        return [
            send(src(j_peer(p)), dst, j_send.at[n, p], j_recv.at[n, p], at(y * NJ + j_peer(p)))
            for p in range(1, NJ)
        ]

    def over_z(n, src, dst):
        return [
            send(src(z_peer(p)), dst, z_send.at[n, p], z_recv.at[n, p], at(y * NJ + z_peer(p) * NC + c))
            for p in range(1, NZ)
        ]

    def over_x(n, src, dst):
        return [
            send(src(x_peer(p)), dst, x_send.at[n, p], x_recv.at[n, p], at(s, x_peer(p)))
            for p in range(1, NX)
        ]

    def span(ref, i, size):
        return ref.at[pl.ds(pl.multiple_of(i * size, size), size)]

    def arrived(copies):
        for copy in copies:
            copy.wait_recv()

    barrier = pltpu.get_barrier_semaphore()
    peers = [at(y_peer(p) * NJ + j) for p in range(1, NY)]
    peers += [at(y * NJ + j_peer(p)) for p in range(1, NJ)]
    peers += [at(s, x_peer(p)) for p in range(1, NX)]
    peers += [at(up), at(down)]
    for peer in peers:
        pl.semaphore_signal(barrier, inc=1, device_id=peer, device_id_type=MESH)
    loads = [
        pltpu.make_async_copy(src, dst, in_sems.at[i])
        for i, (src, dst) in enumerate((
            (cot_in, cot), (owners_in, owners), (feats, table.at[pl.ds(HALO, COARSE)]),
            (counts_in, counts), (rows_in, rows), (wt_in, wt),
        ))
    ]
    for load in loads:
        load.start()
    table[pl.ds(HALO + COARSE + HALO, TAB - COARSE - 2 * HALO), :] = jnp.zeros(
        (TAB - COARSE - 2 * HALO, CIN), BF16
    )

    def ones(mask):
        return jnp.where(mask, 1.0, 0.0).astype(BF16)

    square = (TAB, TAB)
    loads[0].wait()
    c1s[...] = nt(ones(iota(square, 0) == iota(square, 1)), cot[...]).reshape(NY, NJ, WIDE).astype(BF16)
    line = iota((TAB, SLOTS), 0)
    loads[1].wait()
    named = (line & (NY - 1)) * NJ + (line >> 3) == owners[...]
    earlier = ones(iota((SLOTS, SLOTS), 0) < iota((SLOTS, SLOTS), 1))
    before = nn(ones(named), earlier)
    for r in range(CAP):
        place[pl.ds(r * TAB, TAB), :] = ones(named & (before == r))
    pl.semaphore_wait(barrier, len(peers))

    cot_first = over_y(0, lambda d: c1s.at[d], c1.at[y])
    halo_up = send(
        feats.at[pl.ds(COARSE - HALO, HALO)], table.at[pl.ds(0, HALO)],
        e_send.at[0], e_recv.at[0], at(up),
    )
    halo_down = send(
        feats.at[pl.ds(0, HALO)], table.at[pl.ds(HALO + COARSE, HALO)],
        e_send.at[1], e_recv.at[1], at(down),
    )
    c1[y] = c1s[y]
    for load in loads[2:]:
        load.wait()

    spread = ones(iota((COARSE, SLOTS), 0) == (iota((COARSE, SLOTS), 1) >> 3))
    many = jnp.broadcast_to(counts[...], (8, COARSE)).astype(F32).astype(BF16)
    valid = (iota((1, SLOTS), 1) & 7).astype(F32) < nn(many, spread)[0:1]
    for k in range(KVOL):
        onehot[pl.ds(k * TAB, TAB), :] = ones(line == rows[k])
    to_j = ones(iota(square, 1) == (iota(square, 0) & (NY - 1)) * NJ + (iota(square, 0) >> 3))
    to_y = ones(iota(square, 1) == (iota(square, 0) & (NJ - 1)) * NY + (iota(square, 0) >> 4))

    arrived(cot_first)
    c2s[...] = nn(to_j, c1[...].reshape(NS, WIDE)).reshape(NJ, NY, WIDE).astype(BF16)
    cot_second = over_j(0, lambda d: c2s.at[d], c2.at[j])
    c2[j] = c2s[j]

    arrived([halo_up, halo_down])

    @pl.when(s == 0)
    def _():
        table[pl.ds(0, HALO), :] = jnp.zeros((HALO, CIN), BF16)

    @pl.when(s == NS - 1)
    def _():
        table[pl.ds(HALO + COARSE, HALO), :] = jnp.zeros((HALO, CIN), BF16)

    features = table[...]
    high, low = split(nt(wt[...], features))
    for k in range(KVOL):
        zz[pl.ds(0, COUT), pl.ds(k * TAB, TAB)] = high[k * COUT:(k + 1) * COUT]
        zz[pl.ds(COUT, COUT), pl.ds(k * TAB, TAB)] = low[k * COUT:(k + 1) * COUT]
    both = nn(zz[...], onehot[...])
    slot_out = jnp.where(valid, both[:COUT] + both[COUT:], 0.0).astype(BF16)
    for r in range(CAP):
        f1s[:, :, pl.ds(r * COUT, COUT)] = (
            nt(place[pl.ds(r * TAB, TAB), :], slot_out).reshape(NJ, NY, COUT).astype(BF16)
        )
    fine_first = over_j(1, lambda d: f1s.at[d], f1.at[j])
    f1[j] = f1s[j]

    arrived(cot_second)
    turned = c2[...].astype(F32).reshape(NS, WIDE).T.astype(BF16)
    turned = jnp.concatenate([turned[r * COUT:(r + 1) * COUT] for r in range(CAP)], axis=1)
    slot_grad = jnp.where(valid, nn(turned, place[...]), 0.0).astype(BF16)
    high, low = split(nt(slot_grad, onehot[...]))
    for k in range(KVOL):
        st[pl.ds(k * COUT, COUT), pl.ds(0, TAB)] = high[:, k * TAB:(k + 1) * TAB]
        st[pl.ds(k * COUT, COUT), pl.ds(TAB, TAB)] = low[:, k * TAB:(k + 1) * TAB]
    twice = jnp.concatenate([features, features], axis=0)

    def half(d):
        value = nn(st[pl.ds(pl.multiple_of(d * HALF, 16), HALF), :], twice)
        core_a[d] = value[:ROWS_A].reshape(NX, NZ * PART, CIN)
        rest = jnp.concatenate([value[ROWS_A:], jnp.zeros((ROWS_A + ROWS_B - HALF, CIN), F32)], axis=0)
        core_b[d] = rest.reshape(NZ, PARTS_B * PART, CIN)

    order = (2, 1, 3, 0)
    half(1 - c)
    reduce_core_a = [
        send(core_a.at[1 - c, x_peer(p)], from_core_a.at[x_peer(p)], p_send.at[0, p], p_recv.at[0, p], at(partner))
        for p in order
    ]
    reduce_core_b = send(core_b.at[1 - c], from_core_b, p_send.at[0, NX], p_recv.at[0, NX], at(partner))
    half(c)
    reduce_x_a = []
    for p, copy in zip(order, reduce_core_a):
        arrived([copy])
        d = x_peer(p)
        x_a[d] = core_a[c, d] + from_core_a[d]
        if p:
            reduce_x_a.append(send(x_a.at[d], from_x_a.at[x], x_send.at[0, p], x_recv.at[0, p], at(s, d)))
    arrived([reduce_core_b])
    z_b[...] = core_b[c] + from_core_b[...]
    reduce_z_b = over_z(0, lambda d: z_b.at[d], from_z_b.at[z])

    total = dot(st[...], wt[...], ((0,), (0,)))
    grad[...] = total[:TAB] + total[TAB:]
    rim_down = send(grad.at[pl.ds(0, HALO)], rim_high, e_send.at[2], e_recv.at[2], at(down))
    rim_up = send(
        grad.at[pl.ds(HALO + COARSE, HALO)], rim_low, e_send.at[3], e_recv.at[3], at(up)
    )
    x_b[NX - 1] = jnp.zeros((PART, CIN), F32)

    arrived(reduce_x_a)
    mine = x_a[x]
    for p in range(1, NX):
        mine = mine + from_x_a[x_peer(p)]
    z_a[...] = mine.reshape(NZ, PART, CIN)
    reduce_z_a = over_z(1, lambda d: z_a.at[d], from_z_a.at[z])

    arrived(reduce_z_b)
    mine = z_b[z]
    for p in range(1, NZ):
        mine = mine + from_z_b[z_peer(p)]
    x_b[pl.ds(0, PARTS_B)] = mine.reshape(PARTS_B, PART, CIN)
    reduce_x_b = over_x(1, lambda d: x_b.at[d], from_x_b.at[x])

    arrived(fine_first)
    f2s[...] = (
        nn(to_y, f1[...].astype(F32).reshape(NS, WIDE).astype(BF16)).astype(BF16).reshape(NY, NJ, WIDE)
    )
    fine_second = over_y(1, lambda d: f2s.at[d], f2.at[y])
    f2[y] = f2s[y]

    arrived(reduce_z_a)
    mine = z_a[z]
    for p in range(1, NZ):
        mine = mine + from_z_a[z_peer(p)]
    y_a[...] = mine
    exchange_y_a = over_y(2, lambda d: y_a, from_y_a.at[y])
    from_y_a[y] = mine

    arrived(reduce_x_b)
    mine = x_b[x]
    for p in range(1, NX):
        mine = mine + from_x_b[x_peer(p)]
    y_b[...] = mine
    exchange_y_b = over_y(3, lambda d: y_b, from_y_b.at[y])
    from_y_b[y] = mine

    arrived([rim_down, rim_up])
    own = grad[pl.ds(HALO, COARSE), :]
    low = rim_low[...] * jnp.where(s == 0, 0.0, 1.0)
    high = rim_high[...] * jnp.where(s == NS - 1, 0.0, 1.0)
    coarse[pl.ds(0, HALO), :] = (own[:HALO] + low).astype(BF16)
    coarse[pl.ds(HALO, COARSE - 2 * HALO), :] = own[HALO:COARSE - HALO].astype(BF16)
    coarse[pl.ds(COARSE - HALO, HALO), :] = (own[COARSE - HALO:] + high).astype(BF16)
    stores = []

    def store(src, dst):
        copy = pltpu.make_async_copy(src, dst, out_sems.at[len(stores)])
        copy.start()
        stores.append(copy)

    store(coarse, coarse_out)

    arrived(exchange_y_a)
    done = from_y_a[0]
    for q in range(1, NY):
        done = done + from_y_a[q]
    done_a[...] = done
    gather_z_a = over_z(2, lambda d: done_a, span(all_z_a, z, PART))
    span(all_z_a, z, PART)[...] = done

    arrived(exchange_y_b)
    done = from_y_b[0]
    for q in range(1, NY):
        done = done + from_y_b[q]
    done_b[...] = done
    gather_x_b = over_x(2, lambda d: done_b, span(all_x_b, x, PART))
    span(all_x_b, x, PART)[...] = done

    arrived(fine_second)
    fine[...] = f2[...].astype(F32).reshape(NS, WIDE).T.astype(BF16)
    store(fine, fine_out)

    arrived(gather_x_b)
    wide_a, wide_b = NZ * PART, PARTS_B * PART
    whole_b = all_x_b.at[pl.ds(0, wide_b)]
    gather_z_b = over_z(3, lambda d: whole_b, span(out_b.at[c], z, wide_b))
    gather_core = [send(whole_b, span(out_b.at[c], z, wide_b), p_send.at[1, NX], p_recv.at[1, NX], at(partner))]
    span(out_b.at[c], z, wide_b)[...] = whole_b[...]

    arrived(gather_z_a)
    gather_x_a = over_x(3, lambda d: all_z_a, span(out_a.at[c], x, wide_a))
    gather_core.append(send(all_z_a, span(out_a.at[c], x, wide_a), p_send.at[1, 0], p_recv.at[1, 0], at(partner)))
    span(out_a.at[c], x, wide_a)[...] = all_z_a[...]
    for p in (1, 7, 2, 6, 3, 5, 4):
        arrived([gather_z_b[p - 1]])
        piece = span(out_b.at[c], (z + NZ - p) % NZ, wide_b)
        gather_core.append(send(piece, piece, p_send.at[1, NX + p], p_recv.at[1, NX + p], at(partner)))
    for p in (1, 3, 2):
        arrived([gather_x_a[p - 1]])
        piece = span(out_a.at[c], (x + NX - p) % NX, wide_a)
        gather_core.append(send(piece, piece, p_send.at[1, p], p_recv.at[1, p], at(partner)))

    def store_half(d):
        store(out_a.at[d], wgrad_out.at[d, pl.ds(0, ROWS_A)])
        store(out_b.at[d, pl.ds(0, HALF - ROWS_A)], wgrad_out.at[d, pl.ds(ROWS_A, HALF - ROWS_A)])

    store_half(c)
    arrived(gather_core)
    store_half(1 - c)
    for copy in started:
        copy.wait_send()
    for copy in stores:
        copy.wait()


def finish_kernel(fine, coarse, wgrad, fine_out, coarse_out, wgrad_out, fine_v, coarse_v, wgrad_v, sems):
    quarter = HALF // 2
    trips = [(coarse, coarse_v, coarse_out), (fine, fine_v, fine_out)]
    for c in range(NC):
        for q in range(2):
            rows = pl.ds(q * quarter, quarter)
            trips.append(tuple(ref.at[c, rows] for ref in (wgrad, wgrad_v, wgrad_out)))
    loads = [pltpu.make_async_copy(a, b, sems.at[0, i]) for i, (a, b, _) in enumerate(trips)]
    stores = [pltpu.make_async_copy(b, c, sems.at[1, i]) for i, (_, b, c) in enumerate(trips)]
    for load in loads:
        load.start()
    for load, copy in zip(loads, stores):
        load.wait()
        copy.start()
    for copy in stores:
        copy.wait()


def on_device(coarse_features, child_counts, neighbour_rows, fine_owners, weights, cotangent):
    sem = pltpu.SemaphoreType.DMA
    hbm = pl.BlockSpec(memory_space=pltpu.HBM)
    fine, coarse, wgrad = pl.pallas_call(
        kernel,
        out_shape=(
            jax.ShapeDtypeStruct((WIDE, NS), BF16),
            jax.ShapeDtypeStruct((COARSE, CIN), BF16),
            jax.ShapeDtypeStruct((NC, HALF, CIN), F32),
        ),
        in_specs=[hbm] * 6,
        out_specs=(hbm,) * 3,
        scratch_shapes=[
            pltpu.VMEM((WIDE, NS), BF16),
            pltpu.VMEM((COARSE, CIN), BF16),
            pltpu.VMEM((NC, ROWS_A, CIN), F32),
            pltpu.VMEM((NC, ROWS_B, CIN), F32),
            pltpu.VMEM((1, COARSE), jnp.int32),
            pltpu.VMEM((KVOL, 1, SLOTS), jnp.int32),
            pltpu.VMEM((1, SLOTS), jnp.int32),
            pltpu.VMEM((ROWS, CIN), BF16),
            pltpu.VMEM((WIDE, NS), BF16),
            pltpu.VMEM((TAB, CIN), BF16),
            pltpu.VMEM((KVOL * TAB, SLOTS), BF16),
            pltpu.VMEM((CAP * TAB, SLOTS), BF16),
            pltpu.VMEM((2 * COUT, KVOL * TAB), BF16),
            pltpu.VMEM((ROWS, 2 * TAB), BF16),
            pltpu.VMEM((NY, NJ, WIDE), BF16),
            pltpu.VMEM((NY, NJ, WIDE), BF16),
            pltpu.VMEM((NJ, NY, WIDE), BF16),
            pltpu.VMEM((NJ, NY, WIDE), BF16),
            pltpu.VMEM((NJ, NY, WIDE), BF16),
            pltpu.VMEM((NJ, NY, WIDE), BF16),
            pltpu.VMEM((NY, NJ, WIDE), BF16),
            pltpu.VMEM((NY, NJ, WIDE), BF16),
            pltpu.VMEM((TAB, CIN), F32),
            pltpu.VMEM((HALO, CIN), F32),
            pltpu.VMEM((HALO, CIN), F32),
            pltpu.VMEM((NC, NX, NZ * PART, CIN), F32),
            pltpu.VMEM((NX, NZ * PART, CIN), F32),
            pltpu.VMEM((NC, NZ, PARTS_B * PART, CIN), F32),
            pltpu.VMEM((NZ, PARTS_B * PART, CIN), F32),
            pltpu.VMEM((NX, NZ * PART, CIN), F32),
            pltpu.VMEM((NX, NZ * PART, CIN), F32),
            pltpu.VMEM((NZ, PART, CIN), F32),
            pltpu.VMEM((NZ, PART, CIN), F32),
            pltpu.VMEM((PART, CIN), F32),
            pltpu.VMEM((NY, PART, CIN), F32),
            pltpu.VMEM((PART, CIN), F32),
            pltpu.VMEM((NZ * PART, CIN), F32),
            pltpu.VMEM((NZ, PARTS_B * PART, CIN), F32),
            pltpu.VMEM((NZ, PARTS_B * PART, CIN), F32),
            pltpu.VMEM((NX, PART, CIN), F32),
            pltpu.VMEM((NX, PART, CIN), F32),
            pltpu.VMEM((PART, CIN), F32),
            pltpu.VMEM((NY, PART, CIN), F32),
            pltpu.VMEM((PART, CIN), F32),
            pltpu.VMEM((NX * PART, CIN), F32),
            sem((4, NY)), sem((4, NY)),
            sem((2, NJ)), sem((2, NJ)),
            sem((4,)), sem((4,)),
            sem((4, NZ)), sem((4, NZ)),
            sem((4, NX)), sem((4, NX)),
            sem((2, NX + NZ)), sem((2, NX + NZ)),
            sem((6,)), sem((6,)),
        ],
        compiler_params=pltpu.CompilerParams(
            collective_id=0, has_side_effects=True, vmem_limit_bytes=58000 * 1024
        ),
        cost_estimate=pl.CostEstimate(flops=2_000_000_000, bytes_accessed=4_000_000, transcendentals=0),
    )(
        coarse_features[0],
        child_counts,
        neighbour_rows.reshape(KVOL, 1, SLOTS),
        fine_owners.reshape(1, SLOTS),
        weights.transpose(0, 2, 1).reshape(ROWS, CIN),
        cotangent[0].transpose(1, 2, 0).reshape(WIDE, NS),
    )
    fine, coarse, wgrad = pl.pallas_call(
        finish_kernel,
        out_shape=(
            jax.ShapeDtypeStruct((WIDE, NS), BF16),
            jax.ShapeDtypeStruct((COARSE, CIN), BF16),
            jax.ShapeDtypeStruct((NC, HALF, CIN), F32),
        ),
        in_specs=[hbm] * 3,
        out_specs=(hbm,) * 3,
        scratch_shapes=[
            pltpu.VMEM((WIDE, NS), BF16),
            pltpu.VMEM((COARSE, CIN), BF16),
            pltpu.VMEM((NC, HALF, CIN), F32),
            sem((2, 6)),
        ],
        compiler_params=pltpu.CompilerParams(vmem_limit_bytes=58000 * 1024),
    )(fine, coarse, wgrad)
    return (
        fine.reshape(CAP, COUT, NS).transpose(2, 0, 1)[None],
        coarse[None],
        wgrad.reshape(KVOL, COUT, CIN).transpose(0, 2, 1),
    )


def solution(mesh):
    return jax.shard_map(
        on_device,
        mesh=mesh,
        in_specs=(
            P("scene", "space", None),
            P("scene", "space"),
            P("scene", None, "space"),
            P("scene", "space", None),
            P(),
            P("scene", "space", None, None),
        ),
        out_specs=(P("scene", "space", None, None), P("scene", "space", None), P()),
        check_vma=False,
    )
```

time: 69.7 us -> 64.3 us (0.923)
  local copies, waits for them, and re-layouts: 4.48 us -> 0 us
  Pallas kernels: 64.3 us -> 63.5 us
    unnamed x16 -> x0, local copies, waits for them, and re-layouts: 4.1 us -> none
    pallas_call x1 -> x2, Pallas kernels: 64.3 us -> 63.5 us  [the longest x1 61.4 us: on_device(): pl.pallas_call(kernel, out_shape=(jax.ShapeDtypeStruct((WIDE, NS), BF16),...]
where the time goes in v2:
time: 64.3 us; the launch traced here: 64.1 us
  Pallas kernels  63.5 us (99%)
    pallas_call x1, Pallas kernels, on_device(): pl.pallas_call(kernel, out_shape=(jax.ShapeDtypeStruct((WIDE, NS), BF16),...  61.4 us
    pallas_call x1, Pallas kernels, on_device(): pl.pallas_call(finish_kernel, out_shape=(jax.ShapeDtypeStruct((WIDE, NS),...  2.08 us

profile of v2, /device:TPU:1, one launch (start us, length us, event | category | flops | bytes accessed | tf_op | source)
XLA Modules:
  0.0 64.1 jit_solution(15357188665703286919)
XLA Ops:
  0.6 61.4 %shard_map.85 = (bf16[384,128]{1,0:T(8,128)(2,1)}, bf16[64,128]{1,0:T(8,128)(2,1)}, f32[2,864,128]{2,1,0:T(8,128)}) custom-call(bf16[64,128]{1,0:T(8,128)(2,1)} %bitcast.25, s32[1,64]{1,0:T(1,128)} %counts_in.1, s32[27,1,512]{2,1,0:T(1,128)} %bitcast.24, s32[1,512]{1,0:T(1,128)} %bitcast.27, bf16[1728,128]{1,0:T(8,128)(2,1)} %bitcast.21, ...), custom_call_target="tpu_custom_call" | custom-call | flops 2000000000 | bytes 4000000 | tf_op jit(solution)/shard_map/pallas_call | solution.py:378
  62.0 2.1 %shard_map.86 = (bf16[384,128]{1,0:T(8,128)(2,1)}, bf16[64,128]{1,0:T(8,128)(2,1)}, f32[2,864,128]{2,1,0:T(8,128)}) custom-call(bf16[384,128]{1,0:T(8,128)(2,1)} %get-tuple-element.9.fine, bf16[64,128]{1,0:T(8,128)(2,1)} %get-tuple-element.10.coarse, f32[2,864,128]{2,1,0:T(8,128)} %get-tuple-element.11.wgrad), custom_call_target="tpu_custom_call" | custom-call | tf_op jit(solution)/shard_map/pallas_call | solution.py:453

commit v3 on v2

--- a/solution.py
+++ b/solution.py
@@ -43,9 +43,12 @@
     return lax.broadcasted_iota(jnp.int32, shape, dim)
 
 
+def far_first(n):
+    return sorted(range(1, n), key=lambda p: -min(p, n - p))
+
+
 def kernel(
     feats, counts_in, rows_in, owners_in, wt_in, cot_in,
-    fine_out, coarse_out, wgrad_out,
     fine, coarse, out_a, out_b,
     counts, rows, owners, wt, cot,
     table, onehot, place, zz, st,
@@ -55,7 +58,7 @@
     x_a, from_x_a, z_a, from_z_a, y_a, from_y_a, done_a, all_z_a,
     z_b, from_z_b, x_b, from_x_b, y_b, from_y_b, done_b, all_x_b,
     y_send, y_recv, j_send, j_recv, e_send, e_recv,
-    z_send, z_recv, x_send, x_recv, p_send, p_recv, in_sems, out_sems,
+    z_send, z_recv, x_send, x_recv, p_send, p_recv, in_sems,
 ):
     s, x = lax.axis_index("space"), lax.axis_index("scene")
     y, j = s // NJ, s % NJ
@@ -90,34 +93,34 @@
         return copy
 
     def over_y(n, src, dst):
-        return [
-            send(src(y_peer(p)), dst, y_send.at[n, p], y_recv.at[n, p], at(y_peer(p) * NJ + j))
-            for p in range(1, NY)
-        ]
+        return {
+            p: send(src(y_peer(p)), dst, y_send.at[n, p], y_recv.at[n, p], at(y_peer(p) * NJ + j))
+            for p in far_first(NY)
+        }
 
     def over_j(n, src, dst):
-        return [
-            send(src(j_peer(p)), dst, j_send.at[n, p], j_recv.at[n, p], at(y * NJ + j_peer(p)))
-            for p in range(1, NJ)
-        ]
+        return {
+            p: send(src(j_peer(p)), dst, j_send.at[n, p], j_recv.at[n, p], at(y * NJ + j_peer(p)))
+            for p in far_first(NJ)
+        }
 
     def over_z(n, src, dst):
-        return [
-            send(src(z_peer(p)), dst, z_send.at[n, p], z_recv.at[n, p], at(y * NJ + z_peer(p) * NC + c))
-            for p in range(1, NZ)
-        ]
+        return {
+            p: send(src(z_peer(p)), dst, z_send.at[n, p], z_recv.at[n, p], at(y * NJ + z_peer(p) * NC + c))
+            for p in far_first(NZ)
+        }
 
     def over_x(n, src, dst):
-        return [
-            send(src(x_peer(p)), dst, x_send.at[n, p], x_recv.at[n, p], at(s, x_peer(p)))
-            for p in range(1, NX)
-        ]
+        return {
+            p: send(src(x_peer(p)), dst, x_send.at[n, p], x_recv.at[n, p], at(s, x_peer(p)))
+            for p in far_first(NX)
+        }
 
     def span(ref, i, size):
         return ref.at[pl.ds(pl.multiple_of(i * size, size), size)]
 
     def arrived(copies):
-        for copy in copies:
+        for copy in copies.values() if isinstance(copies, dict) else copies:
             copy.wait_recv()
 
     barrier = pltpu.get_barrier_semaphore()
@@ -146,27 +149,26 @@
     square = (TAB, TAB)
     loads[0].wait()
     c1s[...] = nt(ones(iota(square, 0) == iota(square, 1)), cot[...]).reshape(NY, NJ, WIDE).astype(BF16)
+    pl.semaphore_wait(barrier, len(peers))
+
+    cot_first = over_y(0, lambda d: c1s.at[d], c1.at[y])
+    halo_up = send(
+        feats.at[pl.ds(COARSE - HALO, HALO)], table.at[pl.ds(0, HALO)],
+        e_send.at[0], e_recv.at[0], at(up),
+    )
+    halo_down = send(
+        feats.at[pl.ds(0, HALO)], table.at[pl.ds(HALO + COARSE, HALO)],
+        e_send.at[1], e_recv.at[1], at(down),
+    )
+    c1[y] = c1s[y]
+    for load in loads[1:]:
+        load.wait()
     line = iota((TAB, SLOTS), 0)
-    loads[1].wait()
     named = (line & (NY - 1)) * NJ + (line >> 3) == owners[...]
     earlier = ones(iota((SLOTS, SLOTS), 0) < iota((SLOTS, SLOTS), 1))
     before = nn(ones(named), earlier)
     for r in range(CAP):
         place[pl.ds(r * TAB, TAB), :] = ones(named & (before == r))
-    pl.semaphore_wait(barrier, len(peers))
-
-    cot_first = over_y(0, lambda d: c1s.at[d], c1.at[y])
-    halo_up = send(
-        feats.at[pl.ds(COARSE - HALO, HALO)], table.at[pl.ds(0, HALO)],
-        e_send.at[0], e_recv.at[0], at(up),
-    )
-    halo_down = send(
-        feats.at[pl.ds(0, HALO)], table.at[pl.ds(HALO + COARSE, HALO)],
-        e_send.at[1], e_recv.at[1], at(down),
-    )
-    c1[y] = c1s[y]
-    for load in loads[2:]:
-        load.wait()
 
     spread = ones(iota((COARSE, SLOTS), 0) == (iota((COARSE, SLOTS), 1) >> 3))
     many = jnp.broadcast_to(counts[...], (8, COARSE)).astype(F32).astype(BF16)
@@ -292,14 +294,6 @@
     coarse[pl.ds(0, HALO), :] = (own[:HALO] + low).astype(BF16)
     coarse[pl.ds(HALO, COARSE - 2 * HALO), :] = own[HALO:COARSE - HALO].astype(BF16)
     coarse[pl.ds(COARSE - HALO, HALO), :] = (own[COARSE - HALO:] + high).astype(BF16)
-    stores = []
-
-    def store(src, dst):
-        copy = pltpu.make_async_copy(src, dst, out_sems.at[len(stores)])
-        copy.start()
-        stores.append(copy)
-
-    store(coarse, coarse_out)
 
     arrived(exchange_y_a)
     done = from_y_a[0]
@@ -319,7 +313,6 @@
 
     arrived(fine_second)
     fine[...] = f2[...].astype(F32).reshape(NS, WIDE).T.astype(BF16)
-    store(fine, fine_out)
 
     arrived(gather_x_b)
     wide_a, wide_b = NZ * PART, PARTS_B * PART
@@ -333,62 +326,45 @@
     gather_core.append(send(all_z_a, span(out_a.at[c], x, wide_a), p_send.at[1, 0], p_recv.at[1, 0], at(partner)))
     span(out_a.at[c], x, wide_a)[...] = all_z_a[...]
     for p in (1, 7, 2, 6, 3, 5, 4):
-        arrived([gather_z_b[p - 1]])
+        arrived([gather_z_b[p]])
         piece = span(out_b.at[c], (z + NZ - p) % NZ, wide_b)
         gather_core.append(send(piece, piece, p_send.at[1, NX + p], p_recv.at[1, NX + p], at(partner)))
     for p in (1, 3, 2):
-        arrived([gather_x_a[p - 1]])
+        arrived([gather_x_a[p]])
         piece = span(out_a.at[c], (x + NX - p) % NX, wide_a)
         gather_core.append(send(piece, piece, p_send.at[1, p], p_recv.at[1, p], at(partner)))
-
-    def store_half(d):
-        store(out_a.at[d], wgrad_out.at[d, pl.ds(0, ROWS_A)])
-        store(out_b.at[d, pl.ds(0, HALF - ROWS_A)], wgrad_out.at[d, pl.ds(ROWS_A, HALF - ROWS_A)])
-
-    store_half(c)
     arrived(gather_core)
-    store_half(1 - c)
     for copy in started:
         copy.wait_send()
-    for copy in stores:
-        copy.wait()
-
-
-def finish_kernel(fine, coarse, wgrad, fine_out, coarse_out, wgrad_out, fine_v, coarse_v, wgrad_v, sems):
-    quarter = HALF // 2
-    trips = [(coarse, coarse_v, coarse_out), (fine, fine_v, fine_out)]
+
+
+def finish_kernel(fine, coarse, part_a, part_b, fine_out, coarse_out, wgrad_out, sems):
+    pairs = [(fine, fine_out), (coarse, coarse_out)]
     for c in range(NC):
-        for q in range(2):
-            rows = pl.ds(q * quarter, quarter)
-            trips.append(tuple(ref.at[c, rows] for ref in (wgrad, wgrad_v, wgrad_out)))
-    loads = [pltpu.make_async_copy(a, b, sems.at[0, i]) for i, (a, b, _) in enumerate(trips)]
-    stores = [pltpu.make_async_copy(b, c, sems.at[1, i]) for i, (_, b, c) in enumerate(trips)]
-    for load in loads:
-        load.start()
-    for load, copy in zip(loads, stores):
-        load.wait()
+        pairs.append((part_a.at[c], wgrad_out.at[c, pl.ds(0, ROWS_A)]))
+        pairs.append((part_b.at[c, pl.ds(0, HALF - ROWS_A)], wgrad_out.at[c, pl.ds(ROWS_A, HALF - ROWS_A)]))
+    copies = [pltpu.make_async_copy(src, dst, sems.at[i]) for i, (src, dst) in enumerate(pairs)]
+    for copy in copies:
         copy.start()
-    for copy in stores:
+    for copy in copies:
         copy.wait()
 
 
 def on_device(coarse_features, child_counts, neighbour_rows, fine_owners, weights, cotangent):
     sem = pltpu.SemaphoreType.DMA
+    vmem = pl.BlockSpec(memory_space=pltpu.VMEM)
     hbm = pl.BlockSpec(memory_space=pltpu.HBM)
-    fine, coarse, wgrad = pl.pallas_call(
+    fine, coarse, part_a, part_b = pl.pallas_call(
         kernel,
         out_shape=(
             jax.ShapeDtypeStruct((WIDE, NS), BF16),
             jax.ShapeDtypeStruct((COARSE, CIN), BF16),
-            jax.ShapeDtypeStruct((NC, HALF, CIN), F32),
+            jax.ShapeDtypeStruct((NC, ROWS_A, CIN), F32),
+            jax.ShapeDtypeStruct((NC, ROWS_B, CIN), F32),
         ),
         in_specs=[hbm] * 6,
-        out_specs=(hbm,) * 3,
+        out_specs=(vmem,) * 4,
         scratch_shapes=[
-            pltpu.VMEM((WIDE, NS), BF16),
-            pltpu.VMEM((COARSE, CIN), BF16),
-            pltpu.VMEM((NC, ROWS_A, CIN), F32),
-            pltpu.VMEM((NC, ROWS_B, CIN), F32),
             pltpu.VMEM((1, COARSE), jnp.int32),
             pltpu.VMEM((KVOL, 1, SLOTS), jnp.int32),
             pltpu.VMEM((1, SLOTS), jnp.int32),
@@ -436,20 +412,23 @@
             sem((4, NZ)), sem((4, NZ)),
             sem((4, NX)), sem((4, NX)),
             sem((2, NX + NZ)), sem((2, NX + NZ)),
-            sem((6,)), sem((6,)),
+            sem((6,)),
         ],
         compiler_params=pltpu.CompilerParams(
-            collective_id=0, has_side_effects=True, vmem_limit_bytes=58000 * 1024
+            collective_id=0, has_side_effects=True, vmem_limit_bytes=48 * 1024 * 1024
         ),
         cost_estimate=pl.CostEstimate(flops=2_000_000_000, bytes_accessed=4_000_000, transcendentals=0),
-    )(
-        coarse_features[0],
-        child_counts,
-        neighbour_rows.reshape(KVOL, 1, SLOTS),
-        fine_owners.reshape(1, SLOTS),
-        weights.transpose(0, 2, 1).reshape(ROWS, CIN),
-        cotangent[0].transpose(1, 2, 0).reshape(WIDE, NS),
-    )
+    )(*(
+        pltpu.with_memory_space_constraint(operand, pltpu.HBM)
+        for operand in (
+            coarse_features[0],
+            child_counts,
+            neighbour_rows.reshape(KVOL, 1, SLOTS),
+            fine_owners.reshape(1, SLOTS),
+            weights.transpose(0, 2, 1).reshape(ROWS, CIN),
+            cotangent[0].transpose(1, 2, 0).reshape(WIDE, NS),
+        )
+    ))
     fine, coarse, wgrad = pl.pallas_call(
         finish_kernel,
         out_shape=(
@@ -457,16 +436,11 @@
             jax.ShapeDtypeStruct((COARSE, CIN), BF16),
             jax.ShapeDtypeStruct((NC, HALF, CIN), F32),
         ),
-        in_specs=[hbm] * 3,
+        in_specs=[vmem] * 4,
         out_specs=(hbm,) * 3,
-        scratch_shapes=[
-            pltpu.VMEM((WIDE, NS), BF16),
-            pltpu.VMEM((COARSE, CIN), BF16),
-            pltpu.VMEM((NC, HALF, CIN), F32),
-            sem((2, 6)),
-        ],
-        compiler_params=pltpu.CompilerParams(vmem_limit_bytes=58000 * 1024),
-    )(fine, coarse, wgrad)
+        scratch_shapes=[sem((6,))],
+        compiler_params=pltpu.CompilerParams(vmem_limit_bytes=4 * 1024 * 1024),
+    )(fine, coarse, part_a, part_b)
     return (
         fine.reshape(CAP, COUT, NS).transpose(2, 0, 1)[None],
         coarse[None],

time: 64.3 us -> 59.6 us (0.927)
  Pallas kernels: 63.5 us -> 58.8 us
    pallas_call x1, Pallas kernels: 61.4 us -> 57.8 us  [on_device(): pl.pallas_call(kernel, out_shape=(jax.ShapeDtypeStruct((WIDE, NS), BF16),...]
    pallas_call x1, Pallas kernels: 2.08 us -> 1 us  [on_device(): pl.pallas_call(finish_kernel, out_shape=(jax.ShapeDtypeStruct((WIDE, NS),...]
where the time goes in v3:
time: 59.6 us; the launch traced here: 59.4 us
  Pallas kernels  58.8 us (99%)
  between operations  0.64 us (1%)
    pallas_call x1, Pallas kernels, on_device(): pl.pallas_call(kernel, out_shape=(jax.ShapeDtypeStruct((WIDE, NS), BF16),...  57.8 us

profile of v3, /device:TPU:1, one launch (start us, length us, event | category | flops | bytes accessed | tf_op | source)
XLA Modules:
  0.0 59.4 jit_solution(10818719184746939882)
XLA Ops:
  0.6 57.8 %shard_map.85 = (bf16[384,128]{1,0:T(8,128)(2,1)S(1)}, bf16[64,128]{1,0:T(8,128)(2,1)S(1)}, f32[2,512,128]{2,1,0:T(8,128)S(1)}, f32[2,384,128]{2,1,0:T(8,128)S(1)}) custom-call(bf16[64,128]{1,0:T(8,128)(2,1)} %bitcast.25, s32[1,64]{1,0:T(1,128)} %counts_in.1, s32[27,1,512]{2,1,0:T(1,128)} %bitcast.24, s32[1,512]{1,0:T(1,128)} %bitcast.27, ...), custom_call_target="tpu_custom_call" | custom-call | flops 2000000000 | bytes 4000000 | tf_op jit(solution)/shard_map/pallas_call | solution.py:357
  58.4 1.0 %shard_map.86 = (bf16[384,128]{1,0:T(8,128)(2,1)}, bf16[64,128]{1,0:T(8,128)(2,1)}, f32[2,864,128]{2,1,0:T(8,128)}) custom-call(bf16[384,128]{1,0:T(8,128)(2,1)S(1)} %get-tuple-element.10.fine, bf16[64,128]{1,0:T(8,128)(2,1)S(1)} %get-tuple-element.11.coarse, f32[2,512,128]{2,1,0:T(8,128)S(1)} %get-tuple-element.12.part_a, ...), custom_call_target="tpu_custom_call" | custom-call | tf_op jit(solution)/shard_map/pallas_call | solution.py:432

commit v4 on v3

--- a/solution.py
+++ b/solution.py
@@ -13,7 +13,8 @@
 TAB = 128
 WIDE = CAP * COUT
 ROWS = KVOL * COUT
-HALF = ROWS // NC
+KHALF = (KVOL + 1) // NC
+HALF = KHALF * COUT
 PART = 16
 PARTS_B = 3
 ROWS_A = NX * NZ * PART
@@ -51,12 +52,12 @@
     feats, counts_in, rows_in, owners_in, wt_in, cot_in,
     fine, coarse, out_a, out_b,
     counts, rows, owners, wt, cot,
-    table, onehot, place, zz, st,
+    table, onehot, place, found, st,
     c1s, c1, c2s, c2, f1s, f1, f2s, f2,
     grad, rim_low, rim_high,
     core_a, from_core_a, core_b, from_core_b,
     x_a, from_x_a, z_a, from_z_a, y_a, from_y_a, done_a, all_z_a,
-    z_b, from_z_b, x_b, from_x_b, y_b, from_y_b, done_b, all_x_b,
+    y_b, from_y_b, x_b, from_x_b, z_b, from_z_b, done_b, all_x_b,
     y_send, y_recv, j_send, j_recv, e_send, e_recv,
     z_send, z_recv, x_send, x_recv, p_send, p_recv, in_sems,
 ):
@@ -164,12 +165,6 @@
     for load in loads[1:]:
         load.wait()
     line = iota((TAB, SLOTS), 0)
-    named = (line & (NY - 1)) * NJ + (line >> 3) == owners[...]
-    earlier = ones(iota((SLOTS, SLOTS), 0) < iota((SLOTS, SLOTS), 1))
-    before = nn(ones(named), earlier)
-    for r in range(CAP):
-        place[pl.ds(r * TAB, TAB), :] = ones(named & (before == r))
-
     spread = ones(iota((COARSE, SLOTS), 0) == (iota((COARSE, SLOTS), 1) >> 3))
     many = jnp.broadcast_to(counts[...], (8, COARSE)).astype(F32).astype(BF16)
     valid = (iota((1, SLOTS), 1) & 7).astype(F32) < nn(many, spread)[0:1]
@@ -183,6 +178,12 @@
     cot_second = over_j(0, lambda d: c2s.at[d], c2.at[j])
     c2[j] = c2s[j]
 
+    named = (line & (NY - 1)) * NJ + (line >> 3) == owners[...]
+    earlier = ones(iota((SLOTS, SLOTS), 0) < iota((SLOTS, SLOTS), 1))
+    before = nn(ones(named), earlier)
+    for r in range(CAP):
+        place[pl.ds(r * TAB, TAB), :] = ones(named & (before == r))
+
     arrived([halo_up, halo_down])
 
     @pl.when(s == 0)
@@ -194,34 +195,22 @@
         table[pl.ds(HALO + COARSE, HALO), :] = jnp.zeros((HALO, CIN), BF16)
 
     features = table[...]
-    high, low = split(nt(wt[...], features))
+    turned = nt(ones(iota(square, 0) == iota(square, 1)), features).astype(BF16)
     for k in range(KVOL):
-        zz[pl.ds(0, COUT), pl.ds(k * TAB, TAB)] = high[k * COUT:(k + 1) * COUT]
-        zz[pl.ds(COUT, COUT), pl.ds(k * TAB, TAB)] = low[k * COUT:(k + 1) * COUT]
-    both = nn(zz[...], onehot[...])
-    slot_out = jnp.where(valid, both[:COUT] + both[COUT:], 0.0).astype(BF16)
-    for r in range(CAP):
-        f1s[:, :, pl.ds(r * COUT, COUT)] = (
-            nt(place[pl.ds(r * TAB, TAB), :], slot_out).reshape(NJ, NY, COUT).astype(BF16)
-        )
-    fine_first = over_j(1, lambda d: f1s.at[d], f1.at[j])
-    f1[j] = f1s[j]
+        here = pl.ds(k * TAB, TAB)
+        found[here, :] = nn(turned, onehot[here, :]).astype(BF16)
+    found[pl.ds(KVOL * TAB, TAB), :] = jnp.zeros((TAB, SLOTS), BF16)
 
     arrived(cot_second)
     turned = c2[...].astype(F32).reshape(NS, WIDE).T.astype(BF16)
     turned = jnp.concatenate([turned[r * COUT:(r + 1) * COUT] for r in range(CAP)], axis=1)
     slot_grad = jnp.where(valid, nn(turned, place[...]), 0.0).astype(BF16)
-    high, low = split(nt(slot_grad, onehot[...]))
-    for k in range(KVOL):
-        st[pl.ds(k * COUT, COUT), pl.ds(0, TAB)] = high[:, k * TAB:(k + 1) * TAB]
-        st[pl.ds(k * COUT, COUT), pl.ds(TAB, TAB)] = low[:, k * TAB:(k + 1) * TAB]
-    twice = jnp.concatenate([features, features], axis=0)
-
     def half(d):
-        value = nn(st[pl.ds(pl.multiple_of(d * HALF, 16), HALF), :], twice)
-        core_a[d] = value[:ROWS_A].reshape(NX, NZ * PART, CIN)
-        rest = jnp.concatenate([value[ROWS_A:], jnp.zeros((ROWS_A + ROWS_B - HALF, CIN), F32)], axis=0)
-        core_b[d] = rest.reshape(NZ, PARTS_B * PART, CIN)
+        rows_of = pl.ds(pl.multiple_of(d * (KHALF * TAB), 16), KHALF * TAB)
+        value = nt(slot_grad, found[rows_of, :])
+        each = [value[:, k * TAB:(k + 1) * TAB] for k in range(KHALF)]
+        core_a[d] = jnp.concatenate(each[:ROWS_A // COUT], axis=0).reshape(NX, NZ * PART, CIN)
+        core_b[d] = jnp.concatenate(each[ROWS_A // COUT:], axis=0).reshape(NZ, PARTS_B * PART, CIN)
 
     order = (2, 1, 3, 0)
     half(1 - c)
@@ -239,9 +228,22 @@
         if p:
             reduce_x_a.append(send(x_a.at[d], from_x_a.at[x], x_send.at[0, p], x_recv.at[0, p], at(s, d)))
     arrived([reduce_core_b])
-    z_b[...] = core_b[c] + from_core_b[...]
-    reduce_z_b = over_z(0, lambda d: z_b.at[d], from_z_b.at[z])
-
+    y_b[...] = core_b[c] + from_core_b[...]
+    reduce_y_b = over_y(3, lambda d: y_b.at[d], from_y_b.at[y])
+    kernels = jnp.concatenate([wt[pl.ds(k * COUT, COUT), :] for k in range(KVOL)], axis=1)
+    totals = nn(kernels, found[pl.ds(0, KVOL * TAB), :])
+    slot_out = jnp.where(valid, totals, 0.0).astype(BF16)
+    for r in range(CAP):
+        f1s[:, :, pl.ds(r * COUT, COUT)] = (
+            nt(place[pl.ds(r * TAB, TAB), :], slot_out).reshape(NJ, NY, COUT).astype(BF16)
+        )
+    fine_first = over_j(1, lambda d: f1s.at[d], f1.at[j])
+    f1[j] = f1s[j]
+
+    high, low = split(nt(slot_grad, onehot[...]))
+    for k in range(KVOL):
+        st[pl.ds(k * COUT, COUT), pl.ds(0, TAB)] = high[:, k * TAB:(k + 1) * TAB]
+        st[pl.ds(k * COUT, COUT), pl.ds(TAB, TAB)] = low[:, k * TAB:(k + 1) * TAB]
     total = dot(st[...], wt[...], ((0,), (0,)))
     grad[...] = total[:TAB] + total[TAB:]
     rim_down = send(grad.at[pl.ds(0, HALO)], rim_high, e_send.at[2], e_recv.at[2], at(down))
@@ -257,10 +259,10 @@
     z_a[...] = mine.reshape(NZ, PART, CIN)
     reduce_z_a = over_z(1, lambda d: z_a.at[d], from_z_a.at[z])
 
-    arrived(reduce_z_b)
-    mine = z_b[z]
-    for p in range(1, NZ):
-        mine = mine + from_z_b[z_peer(p)]
+    arrived(reduce_y_b)
+    mine = y_b[y]
+    for p in range(1, NY):
+        mine = mine + from_y_b[y_peer(p)]
     x_b[pl.ds(0, PARTS_B)] = mine.reshape(PARTS_B, PART, CIN)
     reduce_x_b = over_x(1, lambda d: x_b.at[d], from_x_b.at[x])
 
@@ -283,9 +285,9 @@
     mine = x_b[x]
     for p in range(1, NX):
         mine = mine + from_x_b[x_peer(p)]
-    y_b[...] = mine
-    exchange_y_b = over_y(3, lambda d: y_b, from_y_b.at[y])
-    from_y_b[y] = mine
+    z_b[...] = mine
+    exchange_z_b = over_z(0, lambda d: z_b, from_z_b.at[z])
+    from_z_b[z] = mine
 
     arrived([rim_down, rim_up])
     own = grad[pl.ds(HALO, COARSE), :]
@@ -303,10 +305,10 @@
     gather_z_a = over_z(2, lambda d: done_a, span(all_z_a, z, PART))
     span(all_z_a, z, PART)[...] = done
 
-    arrived(exchange_y_b)
-    done = from_y_b[0]
-    for q in range(1, NY):
-        done = done + from_y_b[q]
+    arrived(exchange_z_b)
+    done = from_z_b[0]
+    for q in range(1, NZ):
+        done = done + from_z_b[q]
     done_b[...] = done
     gather_x_b = over_x(2, lambda d: done_b, span(all_x_b, x, PART))
     span(all_x_b, x, PART)[...] = done
@@ -317,17 +319,17 @@
     arrived(gather_x_b)
     wide_a, wide_b = NZ * PART, PARTS_B * PART
     whole_b = all_x_b.at[pl.ds(0, wide_b)]
-    gather_z_b = over_z(3, lambda d: whole_b, span(out_b.at[c], z, wide_b))
-    gather_core = [send(whole_b, span(out_b.at[c], z, wide_b), p_send.at[1, NX], p_recv.at[1, NX], at(partner))]
-    span(out_b.at[c], z, wide_b)[...] = whole_b[...]
+    gather_y_b = over_y(4, lambda d: whole_b, span(out_b.at[c], y, wide_b))
+    gather_core = [send(whole_b, span(out_b.at[c], y, wide_b), p_send.at[1, NX], p_recv.at[1, NX], at(partner))]
+    span(out_b.at[c], y, wide_b)[...] = whole_b[...]
 
     arrived(gather_z_a)
     gather_x_a = over_x(3, lambda d: all_z_a, span(out_a.at[c], x, wide_a))
     gather_core.append(send(all_z_a, span(out_a.at[c], x, wide_a), p_send.at[1, 0], p_recv.at[1, 0], at(partner)))
     span(out_a.at[c], x, wide_a)[...] = all_z_a[...]
     for p in (1, 7, 2, 6, 3, 5, 4):
-        arrived([gather_z_b[p]])
-        piece = span(out_b.at[c], (z + NZ - p) % NZ, wide_b)
+        arrived([gather_y_b[p]])
+        piece = span(out_b.at[c], (y + NY - p) % NY, wide_b)
         gather_core.append(send(piece, piece, p_send.at[1, NX + p], p_recv.at[1, NX + p], at(partner)))
     for p in (1, 3, 2):
         arrived([gather_x_a[p]])
@@ -341,8 +343,9 @@
 def finish_kernel(fine, coarse, part_a, part_b, fine_out, coarse_out, wgrad_out, sems):
     pairs = [(fine, fine_out), (coarse, coarse_out)]
     for c in range(NC):
-        pairs.append((part_a.at[c], wgrad_out.at[c, pl.ds(0, ROWS_A)]))
-        pairs.append((part_b.at[c, pl.ds(0, HALF - ROWS_A)], wgrad_out.at[c, pl.ds(ROWS_A, HALF - ROWS_A)]))
+        rest = min(ROWS_B, ROWS - c * HALF - ROWS_A)
+        pairs.append((part_a.at[c], wgrad_out.at[pl.ds(c * HALF, ROWS_A)]))
+        pairs.append((part_b.at[c, pl.ds(0, rest)], wgrad_out.at[pl.ds(c * HALF + ROWS_A, rest)]))
     copies = [pltpu.make_async_copy(src, dst, sems.at[i]) for i, (src, dst) in enumerate(pairs)]
     for copy in copies:
         copy.start()
@@ -373,7 +376,7 @@
             pltpu.VMEM((TAB, CIN), BF16),
             pltpu.VMEM((KVOL * TAB, SLOTS), BF16),
             pltpu.VMEM((CAP * TAB, SLOTS), BF16),
-            pltpu.VMEM((2 * COUT, KVOL * TAB), BF16),
+            pltpu.VMEM((NC * KHALF * TAB, SLOTS), BF16),
             pltpu.VMEM((ROWS, 2 * TAB), BF16),
             pltpu.VMEM((NY, NJ, WIDE), BF16),
             pltpu.VMEM((NY, NJ, WIDE), BF16),
@@ -406,7 +409,7 @@
             pltpu.VMEM((NY, PART, CIN), F32),
             pltpu.VMEM((PART, CIN), F32),
             pltpu.VMEM((NX * PART, CIN), F32),
-            sem((4, NY)), sem((4, NY)),
+            sem((5, NY)), sem((5, NY)),
             sem((2, NJ)), sem((2, NJ)),
             sem((4,)), sem((4,)),
             sem((4, NZ)), sem((4, NZ)),
@@ -434,7 +437,7 @@
         out_shape=(
             jax.ShapeDtypeStruct((WIDE, NS), BF16),
             jax.ShapeDtypeStruct((COARSE, CIN), BF16),
-            jax.ShapeDtypeStruct((NC, HALF, CIN), F32),
+            jax.ShapeDtypeStruct((ROWS, CIN), F32),
         ),
         in_specs=[vmem] * 4,
         out_specs=(hbm,) * 3,

time: 59.6 us -> 58.1 us (0.975)
  Pallas kernels: 58.8 us -> 57.4 us
    pallas_call x1, Pallas kernels: 57.8 us -> 56.4 us  [on_device(): pl.pallas_call(kernel, out_shape=(jax.ShapeDtypeStruct((WIDE, NS), BF16),...]
where the time goes in v4:
time: 58.1 us; the launch traced here: 58 us
  Pallas kernels  57.4 us (99%)
  between operations  0.64 us (1%)
    pallas_call x1, Pallas kernels, on_device(): pl.pallas_call(kernel, out_shape=(jax.ShapeDtypeStruct((WIDE, NS), BF16),...  56.4 us

profile of v4, /device:TPU:1, one launch (start us, length us, event | category | flops | bytes accessed | tf_op | source)
XLA Modules:
  0.0 58.0 jit_solution(4183223520995578880)
XLA Ops:
  0.6 56.4 %shard_map.85 = (bf16[384,128]{1,0:T(8,128)(2,1)S(1)}, bf16[64,128]{1,0:T(8,128)(2,1)S(1)}, f32[2,512,128]{2,1,0:T(8,128)S(1)}, f32[2,384,128]{2,1,0:T(8,128)S(1)}) custom-call(bf16[64,128]{1,0:T(8,128)(2,1)} %bitcast.25, s32[1,64]{1,0:T(1,128)} %counts_in.1, s32[27,1,512]{2,1,0:T(1,128)} %bitcast.24, s32[1,512]{1,0:T(1,128)} %bitcast.27, ...), custom_call_target="tpu_custom_call" | custom-call | flops 2000000000 | bytes 4000000 | tf_op jit(solution)/shard_map/pallas_call | solution.py:360
  57.0 1.0 %shard_map.86 = (bf16[384,128]{1,0:T(8,128)(2,1)}, bf16[64,128]{1,0:T(8,128)(2,1)}, f32[1728,128]{1,0:T(8,128)}) custom-call(bf16[384,128]{1,0:T(8,128)(2,1)S(1)} %get-tuple-element.10.fine, bf16[64,128]{1,0:T(8,128)(2,1)S(1)} %get-tuple-element.11.coarse, f32[2,512,128]{2,1,0:T(8,128)S(1)} %get-tuple-element.12.part_a, ...), custom_call_target="tpu_custom_call" | custom-call | tf_op jit(solution)/shard_map/pallas_call | solution.py:435

commit v5 on v4

--- a/solution.py
+++ b/solution.py
@@ -214,12 +214,15 @@
 
     order = (2, 1, 3, 0)
     half(1 - c)
+    reduce_core_b = send(core_b.at[1 - c], from_core_b, p_send.at[0, NX], p_recv.at[0, NX], at(partner))
     reduce_core_a = [
         send(core_a.at[1 - c, x_peer(p)], from_core_a.at[x_peer(p)], p_send.at[0, p], p_recv.at[0, p], at(partner))
         for p in order
     ]
-    reduce_core_b = send(core_b.at[1 - c], from_core_b, p_send.at[0, NX], p_recv.at[0, NX], at(partner))
     half(c)
+    arrived([reduce_core_b])
+    y_b[...] = core_b[c] + from_core_b[...]
+    reduce_y_b = over_y(3, lambda d: y_b.at[d], from_y_b.at[y])
     reduce_x_a = []
     for p, copy in zip(order, reduce_core_a):
         arrived([copy])
@@ -227,9 +230,6 @@
         x_a[d] = core_a[c, d] + from_core_a[d]
         if p:
             reduce_x_a.append(send(x_a.at[d], from_x_a.at[x], x_send.at[0, p], x_recv.at[0, p], at(s, d)))
-    arrived([reduce_core_b])
-    y_b[...] = core_b[c] + from_core_b[...]
-    reduce_y_b = over_y(3, lambda d: y_b.at[d], from_y_b.at[y])
     kernels = jnp.concatenate([wt[pl.ds(k * COUT, COUT), :] for k in range(KVOL)], axis=1)
     totals = nn(kernels, found[pl.ds(0, KVOL * TAB), :])
     slot_out = jnp.where(valid, totals, 0.0).astype(BF16)

time: 58.1 us -> 58 us (level)
  no operation moved by 1% of the time
where the time goes in v5:
time: 58 us; the launch traced here: 57.8 us
  Pallas kernels  57.2 us (99%)
  between operations  0.64 us (1%)
    pallas_call x1, Pallas kernels, on_device(): pl.pallas_call(kernel, out_shape=(jax.ShapeDtypeStruct((WIDE, NS), BF16),...  56.2 us

profile of v5, /device:TPU:1, one launch (start us, length us, event | category | flops | bytes accessed | tf_op | source)
XLA Modules:
  0.0 57.8 jit_solution(15803159267697984888)
XLA Ops:
  0.6 56.2 %shard_map.85 = (bf16[384,128]{1,0:T(8,128)(2,1)S(1)}, bf16[64,128]{1,0:T(8,128)(2,1)S(1)}, f32[2,512,128]{2,1,0:T(8,128)S(1)}, f32[2,384,128]{2,1,0:T(8,128)S(1)}) custom-call(bf16[64,128]{1,0:T(8,128)(2,1)} %bitcast.25, s32[1,64]{1,0:T(1,128)} %counts_in.1, s32[27,1,512]{2,1,0:T(1,128)} %bitcast.24, s32[1,512]{1,0:T(1,128)} %bitcast.27, ...), custom_call_target="tpu_custom_call" | custom-call | flops 2000000000 | bytes 4000000 | tf_op jit(solution)/shard_map/pallas_call | solution.py:360
  56.8 1.0 %shard_map.86 = (bf16[384,128]{1,0:T(8,128)(2,1)}, bf16[64,128]{1,0:T(8,128)(2,1)}, f32[1728,128]{1,0:T(8,128)}) custom-call(bf16[384,128]{1,0:T(8,128)(2,1)S(1)} %get-tuple-element.10.fine, bf16[64,128]{1,0:T(8,128)(2,1)S(1)} %get-tuple-element.11.coarse, f32[2,512,128]{2,1,0:T(8,128)S(1)} %get-tuple-element.12.part_a, ...), custom_call_target="tpu_custom_call" | custom-call | tf_op jit(solution)/shard_map/pallas_call | solution.py:435
